TPU v7x, 32 devices: a whole 2x2x4 slice. The times are simulated.
32 devices in a mesh: case: 2 (over y), wall: 4 (over z), azim: 4 (over x, core).
Axes of the slice: x: 2, y: 2, z: 4, core: 2. Of those that a mesh axis runs over, the one named last changes fastest.
Arguments:
- state: float32 [12, 2, 32, 512], P(None, 'case', 'wall', 'azim'), parts along dimension 1, may hold values from 0.5 to 1.5
- courant: float32 [2, 32, 512], P('case', 'wall', 'azim'), parts along dimension 0, may hold values from -0.6 to 0.6
- cross_sections: float32 [64], replicated, may hold values from 0.02 to 0.6
- band_fractions: float32 [64], replicated, may hold values from 0.02 to 0.2
- absorb_index: int32 [11, 16], replicated, may hold values from 0 to 63
- band_index: int32 [16], replicated, may hold values from 0 to 63
Outputs:
- new_state: float32 [12, 2, 32, 512], P(None, 'case', 'wall', 'azim'), parts along dimension 1
- wall_flux: float32 [2, 512], P('case', 'azim'), parts along dimension 0
There are 2 independent parts, one for each index of `case`. A program takes and returns all parts, laid end to end along the dimension named above; an argument that names none is the same for every part. Nothing has to cross between parts.
All inputs are finite; a program needn't handle non-finite values.
Results may differ from a plain program's by a relative error of at most 0.0003.
Values sent between devices are 32-bit elements; how exact they have to be, the bound alone decides.
A program may use at most 64 MiB of HBM per device.

v0:
```python
import jax
import jax.numpy as jnp
from jax import lax
from jax.sharding import PartitionSpec as P

KERNEL_WEIGHTS = (0.55, 0.45)
KERNEL_RATES = (1.15, 3.4)
FILTER_STRENGTH = 0.02
COUPLING = 0.1


def with_halo(block, sides, width):
    for axis, dim in sides:
        count = lax.axis_size(axis)
        forward = [(i, i + 1) for i in range(count - 1)]
        forward.append((count - 1, 0))
        backward = [(target, source) for source, target in forward]
        low = lax.ppermute(
            lax.slice_in_dim(block, block.shape[dim] - width, None, axis=dim), axis, forward
        )
        high = lax.ppermute(lax.slice_in_dim(block, 0, width, axis=dim), axis, backward)
        block = jnp.concatenate([low, block, high], axis=dim)
    return block


def band_tables(absorb_index, band_index, cross_sections, band_fractions):
    entries = cross_sections.shape[0]
    table_slots = lax.broadcasted_iota(jnp.int32, (1, 1, entries), 2)
    spectral_absorber_area = jnp.sum(
        jnp.where(absorb_index[:, :, None] == table_slots, cross_sections[None, None, :], 0.0),
        axis=2,
    )
    chosen_values = jnp.where(band_index[:, None] == table_slots[0], band_fractions[None, :], 0.0)
    return (spectral_absorber_area, jnp.sum(chosen_values, axis=1))


def viewing_line_irradiance(
    kinetic_heat_level,
    species_concentrations,
    spectral_absorber_area,
    spectral_fraction_weight,
    mesh_cell_width,
    viewing_line_dimension,
):
    absorption = jnp.einsum(
        "kb,kij->bij",
        spectral_absorber_area,
        species_concentrations,
        precision=lax.Precision.HIGHEST,
    )
    optical_thickness_step = absorption * mesh_cell_width
    optical_depth = (
        lax.cumsum(optical_thickness_step, viewing_line_dimension) - 0.5 * optical_thickness_step
    )
    radiated_energy_rate = (
        spectral_fraction_weight[:, None, None]
        * kinetic_heat_level[None] ** 4
        * optical_thickness_step
    )
    net_flux = 0.0
    wall_flux = 0.0
    for weight, decay_rate in zip(KERNEL_WEIGHTS, KERNEL_RATES):
        growth = jnp.exp(decay_rate * optical_depth)
        falloff = jnp.exp(-decay_rate * optical_depth)
        upward = falloff * lax.cumsum(radiated_energy_rate * growth, viewing_line_dimension)
        tail_sum = lax.cumsum(radiated_energy_rate * falloff, viewing_line_dimension, reverse=True)
        net_flux = net_flux + weight * jnp.sum(upward - growth * tail_sum, axis=0)
        wall_flux = wall_flux + weight * jnp.sum(
            lax.index_in_dim(tail_sum, 0, viewing_line_dimension, keepdims=False), axis=0
        )
    return (net_flux, wall_flux)


def edge_pad(net_flux, viewing_line_dimension):
    count = net_flux.shape[viewing_line_dimension]
    first_row = lax.slice_in_dim(net_flux, 0, 1, axis=viewing_line_dimension)
    last_row = lax.slice_in_dim(net_flux, count - 1, count, axis=viewing_line_dimension)
    return jnp.concatenate([first_row, net_flux, last_row], viewing_line_dimension)


def divergence(padded, viewing_line_dimension, mesh_cell_width):
    count = padded.shape[viewing_line_dimension] - 2
    before = lax.slice_in_dim(padded, 0, count, axis=viewing_line_dimension)
    after = lax.slice_in_dim(padded, 2, count + 2, axis=viewing_line_dimension)
    return (before - after) / (2.0 * mesh_cell_width)


def tendency(shifted, courant, heating):
    gradient = (
        45.0 * (shifted(1) - shifted(-1))
        - 9.0 * (shifted(2) - shifted(-2))
        + (shifted(3) - shifted(-3))
    ) / 60.0
    smoothing = (
        shifted(-3)
        + shifted(3)
        - 6.0 * (shifted(-2) + shifted(2))
        + 15.0 * (shifted(-1) + shifted(1))
        - 20.0 * shifted(0)
    )
    change_sum = FILTER_STRENGTH * smoothing - courant[None] * gradient
    return change_sum.at[0].add(COUPLING * heating)


def radiate(current, spectral_absorber_area, spectral_fraction_weight, mesh_cell_width):
    components, stations, row_count, col_count = current.shape
    line_data = jnp.transpose(current, (0, 2, 1, 3)).reshape(
        components, row_count, stations * col_count
    )
    gathered = lax.all_gather(line_data, "wall", axis=1, tiled=True)
    net_flux, wall_flux = viewing_line_irradiance(
        gathered[0],
        gathered[1:],
        spectral_absorber_area,
        spectral_fraction_weight,
        mesh_cell_width,
        1,
    )
    padded = edge_pad(net_flux, 0)
    row_start = lax.axis_index("wall") * row_count
    heating = divergence(
        lax.dynamic_slice_in_dim(padded, row_start, row_count + 2, 0), 0, mesh_cell_width
    )
    heating = jnp.transpose(heating.reshape(row_count, stations, col_count), (1, 0, 2))
    return (heating, wall_flux.reshape(stations, col_count))


def local(state, courant, cross_sections, band_fractions, absorb_index, band_index):
    spectral_absorber_area, spectral_fraction_weight = band_tables(
        absorb_index, band_index, cross_sections, band_fractions
    )
    mesh_cell_width = 1.0 / (state.shape[2] * lax.axis_size("wall"))
    col_count = state.shape[3]

    def segment_change(current):
        heating, wall_flux = radiate(
            current, spectral_absorber_area, spectral_fraction_weight, mesh_cell_width
        )
        padded = with_halo(current, (("azim", 3),), 3)

        def shifted(offset):
            return lax.slice_in_dim(padded, 3 + offset, 3 + offset + col_count, axis=3)

        return (tendency(shifted, courant, heating), wall_flux)

    first_change, first_flux = segment_change(state)
    middle = state + first_change
    second_change, second_flux = segment_change(middle)
    new_state = 0.5 * (state + middle + second_change)
    return (new_state, 0.5 * (first_flux + second_flux))


def solution(mesh):
    return jax.shard_map(
        local,
        mesh=mesh,
        in_specs=(P(None, "case", "wall", "azim"), P("case", "wall", "azim"), P(), P(), P(), P()),
        out_specs=(P(None, "case", "wall", "azim"), P("case", "azim")),
        check_vma=False,
    )
```

profile of v0, /device:TPU:0, one launch (start us, length us, event | category | flops | bytes accessed | tf_op | source)
XLA Modules:
  0.0 42.3 jit_solution(989441874617617582)
XLA Ops:
  0.6 1.0 %fusion.71 = (f32[12,1,8,3]{3,2,1,0:T(8,128)S(1)}, f32[12,1,8,3]{3,2,1,0:T(8,128)S(1)}) fusion(f32[12,1,8,128]{3,2,1,0:T(8,128)} %param.10), kind=kLoop, calls=%fused_computation.127 | loop fusion | bytes 4608 | tf_op jit(solution)/shard_map/slice | solution.py:21
  1.6 2.4 %collective-permute-start.1 = (f32[12,1,8,3]{3,2,1,0:T(8,128)S(1)}, f32[12,1,8,3]{3,2,1,0:T(8,128)S(1)}, u32[]{:S(2)}, u32[]{:S(2)}) collective-permute-start(f32[12,1,8,3]{3,2,1,0:T(8,128)S(1)} %get-tuple-element.34), channel_id=1, source_target_pairs={{1,0},{2,1},{3,2},{0,3},{5,4},{6,5},{7,6},{4,7},{9,8},{10,9},{11,1... | collective-permute-start | bytes 3464 | tf_op jit(solution)/shard_map/ppermute | solution.py:21
  4.1 14.1 %all-gather = f32[12,1,32,128]{3,1,0,2:T(1,128)S(1)} all-gather(f32[12,1,8,128]{3,1,0,2:T(1,128)S(1)} %copy.53), channel_id=2, replica_groups=mesh['case'=2,'wall'=4,'azim'=4] {'wall'}, dimensions={2}, use_global_device_ids=true | all-gather | bytes 245760 | tf_op jit(solution)/shard_map/all_gather | solution.py:110
  18.3 0.6 %copy-done.1 = s32[11,16]{1,0:T(8,128)S(1)} copy-done((s32[11,16]{1,0:T(8,128)S(1)}, s32[11,16]{1,0:T(8,128)}, u32[]{:S(2)}) %copy-start.1) | copy-done | bytes 728
  19.1 0.4 fusion.5
  19.6 0.6 %copy-done.4 = f32[64]{0:T(128)S(1)} copy-done((f32[64]{0:T(128)S(1)}, f32[64]{0:T(128)}, u32[]{:S(2)}) %copy-start.4) | copy-done | bytes 280
  20.2 0.2 select_reduce_fusion.1
  20.4 0.2 fusion.16
  20.7 0.2 fusion.21
  20.9 0.2 fusion.74
  21.1 0.2 fusion.75
  21.4 0.7 %copy-done.2 = f32[1,8,128]{2,1,0:T(8,128)S(1)} copy-done((f32[1,8,128]{2,1,0:T(8,128)S(1)}, f32[1,8,128]{2,1,0:T(8,128)}, u32[]{:S(2)}) %copy-start.2) | copy-done | bytes 4120
  22.5 13.8 %all-gather.1 = f32[12,1,32,128]{3,1,0,2:T(1,128)S(1)} all-gather(f32[12,1,8,128]{3,1,0,2:T(1,128)S(1)} %copy.56), channel_id=3, replica_groups=mesh['case'=2,'wall'=4,'azim'=4] {'wall'}, dimensions={2}, use_global_device_ids=true | all-gather | bytes 245760 | tf_op jit(solution)/shard_map/all_gather | solution.py:110
  36.4 0.4 fusion.4
  36.8 0.2 fusion.6
  37.1 0.2 fusion.11
  37.3 0.2 fusion.76
  37.6 0.2 fusion.77
  37.9 0.5 %collective-permute-start.2 = (f32[12,1,8,3]{3,2,1,0:T(8,128)S(1)}, f32[12,1,8,3]{3,2,1,0:T(8,128)S(1)}, u32[]{:S(2)}, u32[]{:S(2)}) collective-permute-start(f32[12,1,8,3]{3,2,1,0:T(8,128)S(1)} %get-tuple-element.33), channel_id=1, source_target_pairs={{0,1},{1,2},{2,3},{3,0},{4,5},{5,6},{6,7},{7,4},{8,9},{9,10},{10,1... | collective-permute-start | bytes 3464 | tf_op jit(solution)/shard_map/ppermute | solution.py:18
  38.4 0.5 %multiply_bitcast_fusion.1 = f32[1,128]{1,0:T(1,128)} fusion(f32[128]{0:T(128)S(1)} %get-tuple-element.40, f32[128]{0:T(128)S(1)} %get-tuple-element.41, f32[128]{0:T(128)S(1)} %get-tuple-element.42, f32[128]{0:T(128)S(1)} %get-tuple-element.43), kind=kLoop, calls=%fused_computation.115 | loop fusion | flops 1024 | bytes 2560 | tf_op jit(solution)/shard_map/mul | solution.py:150
  38.9 0.7 %collective-permute-done.3 = f32[12,1,8,3]{3,2,1,0:T(8,128)S(1)} collective-permute-done((f32[12,1,8,3]{3,2,1,0:T(8,128)S(1)}, f32[12,1,8,3]{3,2,1,0:T(8,128)S(1)}, u32[]{:S(2)}, u32[]{:S(2)}) %collective-permute-start.3) | collective-permute-done | bytes 1184 | tf_op jit(solution)/shard_map/ppermute | solution.py:21
  39.7 1.8 %collective-permute-done.2 = f32[12,1,8,3]{3,2,1,0:T(8,128)S(1)} collective-permute-done((f32[12,1,8,3]{3,2,1,0:T(8,128)S(1)}, f32[12,1,8,3]{3,2,1,0:T(8,128)S(1)}, u32[]{:S(2)}, u32[]{:S(2)}) %collective-permute-start.2) | collective-permute-done | bytes 1184 | tf_op jit(solution)/shard_map/ppermute | solution.py:18
  41.5 0.2 multiply_subtract_fusion
  41.7 0.6 %add_multiply_fusion = f32[12,1,8,128]{3,2,1,0:T(8,128)} fusion(f32[12,1,8,128]{3,2,1,0:T(8,128)S(1)} %fusion.55, f32[12,1,8,128]{3,2,1,0:T(8,128)S(1)} %copy-done, f32[12,1,8,128]{3,2,1,0:T(8,128)S(1)} %add.105), kind=kLoop, calls=%fused_computation.75 | loop fusion | flops 36864 | bytes 196608 | tf_op jit(solution)/shard_map/mul | solution.py:149
  (38 shorter events, 1.0 us)
Async XLA Ops:
  0.6 3.4 %copy-start = (f32[12,1,8,128]{3,2,1,0:T(8,128)S(1)}, f32[12,1,8,128]{3,2,1,0:T(8,128)}, u32[]{:S(2)}) copy-start(f32[12,1,8,128]{3,2,1,0:T(8,128)} %param.10) | copy-start | bytes 147460
  1.6 20.5 %collective-permute-start.1 = (f32[12,1,8,3]{3,2,1,0:T(8,128)S(1)}, f32[12,1,8,3]{3,2,1,0:T(8,128)S(1)}, u32[]{:S(2)}, u32[]{:S(2)}) collective-permute-start(f32[12,1,8,3]{3,2,1,0:T(8,128)S(1)} %get-tuple-element.34), channel_id=1, source_target_pairs={{1,0},{2,1},{3,2},{0,3},{5,4},{6,5},{7,6},{4,7},{9,8},{10,9},{11,1... | collective-permute-start | bytes 3464 | tf_op jit(solution)/shard_map/ppermute | solution.py:21
  4.0 18.2 %collective-permute-start = (f32[12,1,8,3]{3,2,1,0:T(8,128)S(1)}, f32[12,1,8,3]{3,2,1,0:T(8,128)S(1)}, u32[]{:S(2)}, u32[]{:S(2)}) collective-permute-start(f32[12,1,8,3]{3,2,1,0:T(8,128)S(1)} %get-tuple-element.35), channel_id=1, source_target_pairs={{0,1},{1,2},{2,3},{3,0},{4,5},{5,6},{6,7},{7,4},{8,9},{9,10},{10,1... | collective-permute-start | bytes 3464 | tf_op jit(solution)/shard_map/ppermute | solution.py:18
  18.2 0.7 %copy-start.1 = (s32[11,16]{1,0:T(8,128)S(1)}, s32[11,16]{1,0:T(8,128)}, u32[]{:S(2)}) copy-start(s32[11,16]{1,0:T(8,128)} %param.14) | copy-start | bytes 2116
  18.2 0.7 %copy-start.3 = (f32[64]{0:T(128)S(1)}, f32[64]{0:T(128)}, u32[]{:S(2)}) copy-start(f32[64]{0:T(128)} %param.12) | copy-start | bytes 772
  19.5 0.7 %copy-start.4 = (f32[64]{0:T(128)S(1)}, f32[64]{0:T(128)}, u32[]{:S(2)}) copy-start(f32[64]{0:T(128)} %param.13) | copy-start | bytes 772
  19.6 0.7 %copy-start.5 = (s32[16]{0:T(128)S(1)}, s32[16]{0:T(128)}, u32[]{:S(2)}) copy-start(s32[16]{0:T(128)} %param.15) | copy-start | bytes 196
  21.4 0.7 %copy-start.2 = (f32[1,8,128]{2,1,0:T(8,128)S(1)}, f32[1,8,128]{2,1,0:T(8,128)}, u32[]{:S(2)}) copy-start(f32[1,8,128]{2,1,0:T(8,128)} %param.11) | copy-start | bytes 12292
  37.8 1.8 %collective-permute-start.3 = (f32[12,1,8,3]{3,2,1,0:T(8,128)S(1)}, f32[12,1,8,3]{3,2,1,0:T(8,128)S(1)}, u32[]{:S(2)}, u32[]{:S(2)}) collective-permute-start(f32[12,1,8,3]{3,2,1,0:T(8,128)S(1)} %get-tuple-element.32), channel_id=1, source_target_pairs={{1,0},{2,1},{3,2},{0,3},{5,4},{6,5},{7,6},{4,7},{9,8},{10,9},{11,1... | collective-permute-start | bytes 3464 | tf_op jit(solution)/shard_map/ppermute | solution.py:21
  37.9 3.6 %collective-permute-start.2 = (f32[12,1,8,3]{3,2,1,0:T(8,128)S(1)}, f32[12,1,8,3]{3,2,1,0:T(8,128)S(1)}, u32[]{:S(2)}, u32[]{:S(2)}) collective-permute-start(f32[12,1,8,3]{3,2,1,0:T(8,128)S(1)} %get-tuple-element.33), channel_id=1, source_target_pairs={{0,1},{1,2},{2,3},{3,0},{4,5},{5,6},{6,7},{7,4},{8,9},{9,10},{10,1... | collective-permute-start | bytes 3464 | tf_op jit(solution)/shard_map/ppermute | solution.py:18
where the time goes:
time: 42.6 us; the launch traced here: 42.3 us
  blocking collectives  27.9 us (65%)
  other arithmetic  4.04 us (9%)
  local copies, waits for them, and re-layouts  3.18 us (7%)
  starting transfers between devices  2.94 us (7%)
  waiting for transfers between devices  2.52 us (6%)
  between operations  0.89 us (2%)
  matrix products  0.84 us (2%)
    all_gather x2, blocking collectives, radiate(): gathered = lax.all_gather(line_data, 'wall', axis=1, tiled=True)  27.9 us
    ppermute x2, starting transfers between devices, with_halo(): lax.ppermute(lax.slice_in_dim(block, 0, width, axis=dim), axis, backward)  2.44 us
    unnamed x14, local copies, waits for them, and re-layouts  2 us
    ppermute x2, waiting for transfers between devices, with_halo(): lax.ppermute(lax.slice_in_dim(block, block.shape[dim] - width, None, axis...  1.79 us
    slice x2, local copies, waits for them, and re-layouts, with_halo(): lax.slice_in_dim(block, 0, width, axis=dim)  1.05 us
    another operation x6, other arithmetic, viewing_line_irradiance(): lax.cumsum(optical_thickness_step, viewing_line_dimension)  1.01 us
    another operation x4, other arithmetic, viewing_line_irradiance(): lax.cumsum(radiated_energy_rate * falloff, viewing_line_dimension, revers...  0.98 us
  transfers between devices with their start and end apart: 4, of which 2 were waited for; matrix products, arithmetic and copies ran while one was open for 6% of the time, Pallas kernels for 0%

commit v1 on v0

--- a/solution.py
+++ b/solution.py
@@ -107,7 +107,15 @@
     line_data = jnp.transpose(current, (0, 2, 1, 3)).reshape(
         components, row_count, stations * col_count
     )
-    gathered = lax.all_gather(line_data, "wall", axis=1, tiled=True)
+    ways, here, step = (lax.axis_size("wall"), lax.axis_index("wall"), line_data.shape[1])
+    line, have = (line_data, 1)
+    while have < ways:
+        line = jnp.concatenate(
+            [line, lax.ppermute(line, "wall", [(d, (d - have) % ways) for d in range(ways)])],
+            axis=1,
+        )
+        have = 2 * have
+    gathered = jnp.roll(line, here * step, axis=1)
     net_flux, wall_flux = viewing_line_irradiance(
         gathered[0],
         gathered[1:],

time: 42.6 us -> 35 us (0.82)
  blocking collectives: 27.9 us -> 0 us
  waiting for transfers between devices: 2.52 us -> 15.8 us
  starting transfers between devices: 2.94 us -> 9.93 us
    all_gather x2 -> x0, blocking collectives: 27.9 us -> none  [radiate(): gathered = lax.all_gather(line_data, 'wall', axis=1, tiled=True)]
    ppermute x0 -> x4, waiting for transfers between devices: none -> 13.3 us  [radiate(): lax.ppermute(line, 'wall', [(d, (d - have) % ways) for d in range(ways)])]
    ppermute x0 -> x4, starting transfers between devices: none -> 8.5 us  [radiate(): lax.ppermute(line, 'wall', [(d, (d - have) % ways) for d in range(ways)])]
    ppermute x2, starting transfers between devices: 2.44 us -> 1.43 us  [with_halo(): lax.ppermute(lax.slice_in_dim(block, 0, width, axis=dim), axis, backward)]
    slice x2, local copies, waits for them, and re-layouts: 1.05 us -> 0.15 us  [with_halo(): lax.slice_in_dim(block, 0, width, axis=dim)]
    ppermute x2, waiting for transfers between devices: 0.73 us -> 0.01 us  [with_halo(): lax.ppermute(lax.slice_in_dim(block, 0, width, axis=dim), axis, backward)]
    ppermute x2, waiting for transfers between devices: 1.79 us -> 2.51 us  [with_halo(): lax.ppermute(lax.slice_in_dim(block, block.shape[dim] - width, None, axis...]
    unnamed x14, local copies, waits for them, and re-layouts: 2 us -> 2.69 us
  transfers between devices with their start and end apart: 4 -> 8, of which waited for: 2 -> 5; matrix products, arithmetic and copies ran while one was open for 6% -> 2% of each run, Pallas kernels for 0% -> 0%
where the time goes in v1:
time: 35 us; the launch traced here: 34.8 us
  waiting for transfers between devices  15.8 us (45%)
  starting transfers between devices  9.93 us (28%)
  other arithmetic  4.44 us (13%)
  local copies, waits for them, and re-layouts  2.87 us (8%)
  between operations  0.9 us (3%)
  matrix products  0.88 us (3%)
    ppermute x4, waiting for transfers between devices, radiate(): lax.ppermute(line, 'wall', [(d, (d - have) % ways) for d in range(ways)])  13.3 us
    ppermute x4, starting transfers between devices, radiate(): lax.ppermute(line, 'wall', [(d, (d - have) % ways) for d in range(ways)])  8.5 us
    unnamed x14, local copies, waits for them, and re-layouts  2.69 us
    ppermute x2, waiting for transfers between devices, with_halo(): lax.ppermute(lax.slice_in_dim(block, block.shape[dim] - width, None, axis...  2.51 us
    ppermute x2, starting transfers between devices, with_halo(): lax.ppermute(lax.slice_in_dim(block, 0, width, axis=dim), axis, backward)  1.43 us
    another operation x6, other arithmetic, viewing_line_irradiance(): lax.cumsum(optical_thickness_step, viewing_line_dimension)  1.01 us
    another operation x4, other arithmetic, viewing_line_irradiance(): lax.cumsum(radiated_energy_rate * falloff, viewing_line_dimension, revers...  0.98 us
    dot_general x2, matrix products, viewing_line_irradiance(): jnp.einsum('kb,kij->bij', spectral_absorber_area, species_concentrations,...  0.88 us
  transfers between devices with their start and end apart: 8, of which 5 were waited for; matrix products, arithmetic and copies ran while one was open for 2% of the time, Pallas kernels for 0%

profile of v1, /device:TPU:0, one launch (start us, length us, event | category | flops | bytes accessed | tf_op | source)
XLA Modules:
  0.0 34.8 jit_solution(11101532687154516964)
XLA Ops:
  0.6 0.9 %copy.47 = f32[12,1,8,128]{3,0,2,1:T(8,128)S(1)} copy(f32[12,1,8,128]{3,2,1,0:T(8,128)} %param.12) | data formatting | bytes 98304 | tf_op args[0]
  1.5 5.1 %collective-permute-start.2 = (f32[12,8,128]{2,0,1:T(8,128)S(1)}, f32[12,8,128]{2,0,1:T(8,128)S(1)}, u32[]{:S(2)}, u32[]{:S(2)}) collective-permute-start(f32[12,8,128]{2,0,1:T(8,128)S(1)} %bitcast.32), channel_id=1, source_target_pairs={{0,12},{4,0},{8,4},{12,8},{1,13},{5,1},{9,5},{13,9},{2,14},{6,2},{... | collective-permute-start | bytes 147464 | tf_op jit(solution)/shard_map/ppermute | solution.py:114
  6.7 0.7 %collective-permute-start.1 = (f32[12,1,8,3]{3,2,1,0:T(8,128)S(1)}, f32[12,1,8,3]{3,2,1,0:T(8,128)S(1)}, u32[]{:S(2)}, u32[]{:S(2)}) collective-permute-start(f32[12,1,8,3]{3,2,1,0:T(8,128)S(1)} %get-tuple-element.33), channel_id=1, source_target_pairs={{1,0},{2,1},{3,2},{0,3},{5,4},{6,5},{7,6},{4,7},{9,8},{10,9},{11,1... | collective-permute-start | bytes 3464 | tf_op jit(solution)/shard_map/ppermute | solution.py:21
  7.4 0.7 %copy-done.2 = f32[1,8,128]{2,1,0:T(8,128)S(1)} copy-done((f32[1,8,128]{2,1,0:T(8,128)S(1)}, f32[1,8,128]{2,1,0:T(8,128)}, u32[]{:S(2)}) %copy-start.2) | copy-done | bytes 4120
  8.1 0.6 %copy-done.4 = f32[64]{0:T(128)S(1)} copy-done((f32[64]{0:T(128)S(1)}, f32[64]{0:T(128)}, u32[]{:S(2)}) %copy-start.4) | copy-done | bytes 280
  8.9 0.5 %copy-done.3 = f32[64]{0:T(128)S(1)} copy-done((f32[64]{0:T(128)S(1)}, f32[64]{0:T(128)}, u32[]{:S(2)}) %copy-start.3) | copy-done | bytes 280
  9.6 0.3 collective-permute-start.3
  9.9 0.9 %collective-permute-done = f32[12,1,8,3]{3,2,1,0:T(8,128)S(1)} collective-permute-done((f32[12,1,8,3]{3,2,1,0:T(8,128)S(1)}, f32[12,1,8,3]{3,2,1,0:T(8,128)S(1)}, u32[]{:S(2)}, u32[]{:S(2)}) %collective-permute-start) | collective-permute-done | bytes 1184 | tf_op jit(solution)/shard_map/ppermute | solution.py:18
  11.1 7.3 %collective-permute-done.3 = f32[12,16,128]{2,0,1:T(8,128)S(1)} collective-permute-done((f32[12,16,128]{2,0,1:T(8,128)S(1)}, f32[12,16,128]{2,0,1:T(8,128)S(1)}, u32[]{:S(2)}, u32[]{:S(2)}) %collective-permute-start.3) | collective-permute-done | bytes 98336 | tf_op jit(solution)/shard_map/ppermute | solution.py:114
  18.3 0.3 fusion.6
  18.7 0.4 %fusion.9 = f32[16,32,128]{2,0,1:T(8,128)S(1)} fusion(f32[12,32,128]{2,0,1:T(8,128)S(1)} %fusion.6, f32[11,16]{1,0:T(8,128)S(1)} %select_reduce_fusion), kind=kOutput, calls=%fused_computation.27 | convolution fusion | flops 8650752 | bytes 459456 | tf_op jit(solution)/shard_map/kb,kij->bij/dot_general | solution.py:45
  19.1 0.2 fusion.23
  19.4 0.2 fusion.28
  20.3 2.2 %collective-permute-start.6 = (f32[12,8,128]{2,1,0:T(8,128)S(1)}, f32[12,8,128]{2,1,0:T(8,128)S(1)}, u32[]{:S(2)}, u32[]{:S(2)}) collective-permute-start(f32[12,8,128]{2,1,0:T(8,128)S(1)} %bitcast.29), channel_id=1, source_target_pairs={{0,12},{4,0},{8,4},{12,8},{1,13},{5,1},{9,5},{13,9},{2,14},{6,2},{... | collective-permute-start | bytes 147464 | tf_op jit(solution)/shard_map/ppermute | solution.py:114
  22.5 0.8 %collective-permute-start.5 = (f32[12,1,8,3]{3,2,1,0:T(8,128)S(1)}, f32[12,1,8,3]{3,2,1,0:T(8,128)S(1)}, u32[]{:S(2)}, u32[]{:S(2)}) collective-permute-start(f32[12,1,8,3]{3,2,1,0:T(8,128)S(1)} %get-tuple-element.31), channel_id=1, source_target_pairs={{1,0},{2,1},{3,2},{0,3},{5,4},{6,5},{7,6},{4,7},{9,8},{10,9},{11,1... | collective-permute-start | bytes 3464 | tf_op jit(solution)/shard_map/ppermute | solution.py:21
  23.3 1.1 %collective-permute-done.6 = f32[12,8,128]{2,1,0:T(8,128)S(1)} collective-permute-done((f32[12,8,128]{2,1,0:T(8,128)S(1)}, f32[12,8,128]{2,1,0:T(8,128)S(1)}, u32[]{:S(2)}, u32[]{:S(2)}) %collective-permute-start.6) | collective-permute-done | bytes 49184 | tf_op jit(solution)/shard_map/ppermute | solution.py:114
  24.4 0.8 %collective-permute-start.7 = (f32[12,16,128]{2,1,0:T(8,128)S(1)}, f32[12,16,128]{2,1,0:T(8,128)S(1)}, u32[]{:S(2)}, u32[]{:S(2)}) collective-permute-start(f32[12,16,128]{2,1,0:T(8,128)S(1)} %pad_maximum_fusion.1), channel_id=1, source_target_pairs={{0,8},{4,12},{8,0},{12,4},{1,9},{5,13},{9,1},{13,5},{2,10},{6,14},... | collective-permute-start | bytes 294920 | tf_op jit(solution)/shard_map/ppermute | solution.py:114
  25.2 1.6 %collective-permute-done.4 = f32[12,1,8,3]{3,2,1,0:T(8,128)S(1)} collective-permute-done((f32[12,1,8,3]{3,2,1,0:T(8,128)S(1)}, f32[12,1,8,3]{3,2,1,0:T(8,128)S(1)}, u32[]{:S(2)}, u32[]{:S(2)}) %collective-permute-start.4) | collective-permute-done | bytes 1184 | tf_op jit(solution)/shard_map/ppermute | solution.py:18
  27.0 4.9 %collective-permute-done.7 = f32[12,16,128]{2,1,0:T(8,128)S(1)} collective-permute-done((f32[12,16,128]{2,1,0:T(8,128)S(1)}, f32[12,16,128]{2,1,0:T(8,128)S(1)}, u32[]{:S(2)}, u32[]{:S(2)}) %collective-permute-start.7) | collective-permute-done | bytes 98336 | tf_op jit(solution)/shard_map/ppermute | solution.py:114
  32.1 0.5 %fusion.11 = f32[16,32,128]{2,0,1:T(8,128)S(1)} fusion(f32[11,32,128]{2,1,0:T(8,128)S(1)} %slice.233, f32[11,16]{1,0:T(8,128)S(1)} %select_reduce_fusion), kind=kOutput, calls=%fused_computation.29 | convolution fusion | flops 8650752 | bytes 443072 | tf_op jit(solution)/shard_map/kb,kij->bij/dot_general | solution.py:45
  32.6 0.2 fusion.13
  32.8 0.2 fusion.18
  33.7 0.6 %add_multiply_fusion = f32[12,1,8,128]{3,2,1,0:T(8,128)} fusion(f32[12,1,8,128]{3,2,1,0:T(8,128)S(1)} %constant_dynamic-update-slice_fusion.2, f32[12,1,8,128]{3,2,1,0:T(8,128)S(1)} %copy-done, f32[12,1,8,128]{3,2,1,0:T(8,128)S(1)} %add.113), kind=kLoop, calls=%fused_computation.100 | loop fusion | flops 36864 | bytes 196608 | tf_op jit(solution)/shard_map/mul | solution.py:157
  34.3 0.5 %multiply_bitcast_fusion.1 = f32[1,128]{1,0:T(1,128)} fusion(f32[128]{0:T(128)S(1)} %get-tuple-element.39, f32[128]{0:T(128)S(1)} %get-tuple-element.40, f32[128]{0:T(128)S(1)} %get-tuple-element.41, f32[128]{0:T(128)S(1)} %get-tuple-element.42), kind=kLoop, calls=%fused_computation.141 | loop fusion | flops 1024 | bytes 2560 | tf_op jit(solution)/shard_map/mul | solution.py:158
  (46 shorter events, 2.2 us)
Async XLA Ops:
  0.6 6.0 %copy-start = (f32[12,1,8,128]{3,2,1,0:T(8,128)S(1)}, f32[12,1,8,128]{3,2,1,0:T(8,128)}, u32[]{:S(2)}) copy-start(f32[12,1,8,128]{3,2,1,0:T(8,128)} %param.12) | copy-start | bytes 147460
  1.5 8.1 %collective-permute-start.2 = (f32[12,8,128]{2,0,1:T(8,128)S(1)}, f32[12,8,128]{2,0,1:T(8,128)S(1)}, u32[]{:S(2)}, u32[]{:S(2)}) collective-permute-start(f32[12,8,128]{2,0,1:T(8,128)S(1)} %bitcast.32), channel_id=1, source_target_pairs={{0,12},{4,0},{8,4},{12,8},{1,13},{5,1},{9,5},{13,9},{2,14},{6,2},{... | collective-permute-start | bytes 147464 | tf_op jit(solution)/shard_map/ppermute | solution.py:114
  6.7 2.9 %collective-permute-start.1 = (f32[12,1,8,3]{3,2,1,0:T(8,128)S(1)}, f32[12,1,8,3]{3,2,1,0:T(8,128)S(1)}, u32[]{:S(2)}, u32[]{:S(2)}) collective-permute-start(f32[12,1,8,3]{3,2,1,0:T(8,128)S(1)} %get-tuple-element.33), channel_id=1, source_target_pairs={{1,0},{2,1},{3,2},{0,3},{5,4},{6,5},{7,6},{4,7},{9,8},{10,9},{11,1... | collective-permute-start | bytes 3464 | tf_op jit(solution)/shard_map/ppermute | solution.py:21
  7.4 3.5 %collective-permute-start = (f32[12,1,8,3]{3,2,1,0:T(8,128)S(1)}, f32[12,1,8,3]{3,2,1,0:T(8,128)S(1)}, u32[]{:S(2)}, u32[]{:S(2)}) collective-permute-start(f32[12,1,8,3]{3,2,1,0:T(8,128)S(1)} %get-tuple-element.34), channel_id=1, source_target_pairs={{0,1},{1,2},{2,3},{3,0},{4,5},{5,6},{6,7},{7,4},{8,9},{9,10},{10,1... | collective-permute-start | bytes 3464 | tf_op jit(solution)/shard_map/ppermute | solution.py:18
  7.4 0.7 %copy-start.2 = (f32[1,8,128]{2,1,0:T(8,128)S(1)}, f32[1,8,128]{2,1,0:T(8,128)}, u32[]{:S(2)}) copy-start(f32[1,8,128]{2,1,0:T(8,128)} %param.13) | copy-start | bytes 12292
  7.4 1.5 %copy-start.1 = (s32[11,16]{1,0:T(8,128)S(1)}, s32[11,16]{1,0:T(8,128)}, u32[]{:S(2)}) copy-start(s32[11,16]{1,0:T(8,128)} %param.16) | copy-start | bytes 2116
  8.0 0.7 %copy-start.4 = (f32[64]{0:T(128)S(1)}, f32[64]{0:T(128)}, u32[]{:S(2)}) copy-start(f32[64]{0:T(128)} %param.15) | copy-start | bytes 772
  8.0 0.7 %copy-start.5 = (s32[16]{0:T(128)S(1)}, s32[16]{0:T(128)}, u32[]{:S(2)}) copy-start(s32[16]{0:T(128)} %param.17) | copy-start | bytes 196
  8.7 0.7 %copy-start.3 = (f32[64]{0:T(128)S(1)}, f32[64]{0:T(128)}, u32[]{:S(2)}) copy-start(f32[64]{0:T(128)} %param.14) | copy-start | bytes 772
  9.6 8.7 %collective-permute-start.3 = (f32[12,16,128]{2,0,1:T(8,128)S(1)}, f32[12,16,128]{2,0,1:T(8,128)S(1)}, u32[]{:S(2)}, u32[]{:S(2)}) collective-permute-start(f32[12,16,128]{2,0,1:T(8,128)S(1)} %pad_maximum_fusion), channel_id=1, source_target_pairs={{0,8},{4,12},{8,0},{12,4},{1,9},{5,13},{9,1},{13,5},{2,10},{6,14},... | collective-permute-start | bytes 294920 | tf_op jit(solution)/shard_map/ppermute | solution.py:114
  20.3 4.1 %collective-permute-start.6 = (f32[12,8,128]{2,1,0:T(8,128)S(1)}, f32[12,8,128]{2,1,0:T(8,128)S(1)}, u32[]{:S(2)}, u32[]{:S(2)}) collective-permute-start(f32[12,8,128]{2,1,0:T(8,128)S(1)} %bitcast.29), channel_id=1, source_target_pairs={{0,12},{4,0},{8,4},{12,8},{1,13},{5,1},{9,5},{13,9},{2,14},{6,2},{... | collective-permute-start | bytes 147464 | tf_op jit(solution)/shard_map/ppermute | solution.py:114
  22.5 2.7 %collective-permute-start.5 = (f32[12,1,8,3]{3,2,1,0:T(8,128)S(1)}, f32[12,1,8,3]{3,2,1,0:T(8,128)S(1)}, u32[]{:S(2)}, u32[]{:S(2)}) collective-permute-start(f32[12,1,8,3]{3,2,1,0:T(8,128)S(1)} %get-tuple-element.31), channel_id=1, source_target_pairs={{1,0},{2,1},{3,2},{0,3},{5,4},{6,5},{7,6},{4,7},{9,8},{10,9},{11,1... | collective-permute-start | bytes 3464 | tf_op jit(solution)/shard_map/ppermute | solution.py:21
  23.3 3.5 %collective-permute-start.4 = (f32[12,1,8,3]{3,2,1,0:T(8,128)S(1)}, f32[12,1,8,3]{3,2,1,0:T(8,128)S(1)}, u32[]{:S(2)}, u32[]{:S(2)}) collective-permute-start(f32[12,1,8,3]{3,2,1,0:T(8,128)S(1)} %get-tuple-element.32), channel_id=1, source_target_pairs={{0,1},{1,2},{2,3},{3,0},{4,5},{5,6},{6,7},{7,4},{8,9},{9,10},{10,1... | collective-permute-start | bytes 3464 | tf_op jit(solution)/shard_map/ppermute | solution.py:18
  24.4 7.6 %collective-permute-start.7 = (f32[12,16,128]{2,1,0:T(8,128)S(1)}, f32[12,16,128]{2,1,0:T(8,128)S(1)}, u32[]{:S(2)}, u32[]{:S(2)}) collective-permute-start(f32[12,16,128]{2,1,0:T(8,128)S(1)} %pad_maximum_fusion.1), channel_id=1, source_target_pairs={{0,8},{4,12},{8,0},{12,4},{1,9},{5,13},{9,1},{13,5},{2,10},{6,14},... | collective-permute-start | bytes 294920 | tf_op jit(solution)/shard_map/ppermute | solution.py:114
